TPU v7x, 512 devices: a whole 4x4x16 slice. The times are simulated.
512 devices in a mesh: pop: 64 (over y_lo, z, core), shard: 8 (over x, y_hi).
Axes of the slice: x: 4, y: 4 (y_hi: 2, y_lo: 2; y = y_hi * 2 + y_lo), z: 16, core: 2. Of those that a mesh axis runs over, the one named last changes fastest.
Arguments:
- hidden: bfloat16 [8192, 4096], P('pop'), may hold values from -6 to 6
- weight: bfloat16 [4096, 14336], P('pop', 'shard'), may hold values from -0.09375 to 0.09375
- left_factors: bfloat16 [512, 4096], P('pop'), may hold values from -6 to 6
- right_factors: bfloat16 [512, 14336], P('pop', 'shard'), may hold values from -6 to 6
- target: bfloat16 [8192, 14336], P('pop', 'shard'), may hold values from -6 to 6
Outputs:
- up_out: bfloat16 [8192, 14336], P('pop', 'shard')
- step: float32 [4096, 14336], P('pop', 'shard')
- fitness: float32 [512], P('pop')
All inputs are finite; a program needn't handle non-finite values.
Results may differ from a plain program's by a relative error of at most 0.001.
Values may be sent and summed in bfloat16 or wider, within the bound.
No kernel may reach another device: no remote copies, remote signals or barrier semaphores. Data moves between devices by JAX's collectives and lax.ppermute only.
A program may use at most 64 MiB of HBM per device.

v0:
```python
import math
import jax
import jax.numpy as jnp
from jax import lax
from jax.sharding import PartitionSpec as P

noise_scale = 0.5
spread_eps = 1e-05


def split_parts(values):
    high = values.astype(jnp.bfloat16)
    kept = lax.optimization_barrier(high)
    low = (values - kept.astype(jnp.float32)).astype(jnp.bfloat16)
    return (high, low)


def local(hidden, weight, left_factors, right_factors, target):
    local_members = left_factors.shape[0]
    row_count = hidden.shape[0]
    token_count = row_count // local_members
    feature_count = hidden.shape[1]
    local_cols = weight.shape[1]
    member_count = local_members * lax.axis_size("pop")
    base_out = jnp.dot(
        hidden,
        lax.all_gather(weight, "pop", axis=0, tiled=True),
        preferred_element_type=jnp.float32,
    )
    grouped = hidden.reshape(local_members, token_count, feature_count)
    projected = jnp.einsum(
        "mtd,md->mt", grouped, left_factors, preferred_element_type=jnp.float32
    ) / math.sqrt(feature_count)
    right_wide = right_factors.astype(jnp.float32)
    perturbed = (
        base_out.reshape(local_members, token_count, local_cols)
        + noise_scale * projected[:, :, None] * right_wide[:, None, :]
    )
    up_out = perturbed.astype(jnp.bfloat16).reshape(row_count, local_cols)
    directions = target.reshape(local_members, token_count, local_cols).astype(jnp.float32)
    partial_value = jnp.sum(jax.nn.silu(perturbed) * directions, axis=(1, 2))
    reward = lax.psum(partial_value, "shard")
    mean_reward = lax.psum(jnp.sum(reward), "pop") / member_count
    centered = reward - mean_reward
    spread = lax.psum(jnp.sum(centered * centered), "pop") / member_count
    fitness = (reward - mean_reward) / jnp.sqrt(spread + spread_eps)
    weighted = left_factors.astype(jnp.float32) * fitness[:, None]
    weighted_all = lax.all_to_all(weighted, "pop", split_axis=1, concat_axis=0, tiled=True)
    weighted_high, weighted_low = split_parts(weighted_all)
    contract = (((0,), (0,)), ((), ()))
    portion = lax.all_gather(right_factors, "pop", axis=0, tiled=True)
    upper = lax.dot_general(weighted_high, portion, contract, preferred_element_type=jnp.float32)
    lower = lax.dot_general(weighted_low, portion, contract, preferred_element_type=jnp.float32)
    summed = upper + lower
    step = summed / math.sqrt(member_count)
    return (up_out, step, fitness)


def solution(mesh):
    in_specs = (
        P("pop", None),
        P("pop", "shard"),
        P("pop", None),
        P("pop", "shard"),
        P("pop", "shard"),
    )
    out_specs = (P("pop", "shard"), P("pop", "shard"), P("pop"))
    return jax.shard_map(local, mesh=mesh, in_specs=in_specs, out_specs=out_specs, check_vma=False)
```

profile of v0, /device:TPU:1, one launch (start us, length us, event | category | flops | bytes accessed | tf_op | source)
XLA Modules:
  0.0 432.2 jit_solution(2508791868741130458)
XLA Ops:
  7.2 0.7 all-gather.3.cloned.1.call-update
  8.0 0.7 all-gather.5.cloned.1.call-update
  8.7 0.8 convert_element_type.23
  9.4 1.3 fusion.3
  10.8 0.1 mul.48
  10.8 0.1 bitcast_multiply_fusion
  11.0 142.6 %all-gather.3.cloned.1.call-done = bf16[4096,1792]{1,0:T(8,128)(2,1)} async-done(((bf16[64,1792]{1,0:T(8,128)(2,1)}), bf16[4096,1792]{1,0:T(8,128)(2,1)}) %all-gather.3.cloned.1.call-update) | async-done | bytes 14680080 | tf_op jit(solution)/shard_map/all_gather | solution.py:27
  153.6 8.3 %multiply_reduce_fusion = (f32[128]{0:T(128)S(1)}, bf16[128,1792]{1,0:T(8,128)(2,1)}) fusion(bf16[128,1792]{1,0:T(8,128)(2,1)S(1)} %copy-done.4, f32[128,1792]{1,0:T(8,128)S(1)} %bitcast_multiply_fusion, bf16[128,4096]{1,0:T(8,128)(2,1)S(1)} %copy-done, bf16[4096,1792]{1,0:T(8,128)(2,1)} %all-gather.3.cloned.1.call-done), kind=kOutput, calls=%fused_computation.4 | convolution fusion | flops 1881112448 | bytes 17564160 | tf_op jit(solution)/shard_map/dot_general | solution.py:25
  161.9 0.1 reduce_sum.35
  161.9 0.1 reduce_sum.36
  162.1 20.1 %psum.21 = f32[8]{0:T(128)S(1)} all-reduce(f32[8]{0:T(128)S(1)} %reduce_sum.36), channel_id=1, replica_groups=mesh['pop'=64,'shard'=8] {'shard'}, use_global_device_ids=true, to_apply=%region_2.3 | all-reduce | flops 8 | bytes 64 | tf_op jit(solution)/shard_map/psum | solution.py:42
  182.2 0.6 reduce_sum.37
  182.8 108.7 %psum.22 = f32[]{:T(128)} all-reduce(f32[]{:T(128)} %reduce_sum.37), channel_id=1, replica_groups=mesh['pop'=64,'shard'=8] {'pop'}, use_global_device_ids=true, to_apply=%region_4.5 | all-reduce | flops 1 | bytes 8 | tf_op jit(solution)/shard_map/psum | solution.py:43
  292.1 0.6 multiply_reduce_fusion.1
  292.7 105.3 %psum.23 = f32[]{:T(128)} all-reduce(f32[]{:T(128)} %multiply_reduce_fusion.1), channel_id=1, replica_groups=mesh['pop'=64,'shard'=8] {'pop'}, use_global_device_ids=true, to_apply=%region_6.7 | all-reduce | flops 1 | bytes 8 | tf_op jit(solution)/shard_map/psum | solution.py:45
  398.8 0.1 all_to_all.14
  398.9 0.2 copy.14
  399.1 0.2 reshape.28
  399.3 21.1 %all_to_all.19 = f32[64,1,512]{2,1,0:T(1,128)S(1)} all-to-all(f32[64,1,512]{2,1,0:T(1,128)S(1)} %reshape.28), channel_id=1, replica_groups=mesh['pop'=64,'shard'=8] {'pop'}, dimensions={0} | all-to-all | bytes 262144 | tf_op jit(solution)/shard_map/all_to_all | solution.py:48
  420.4 0.5 broadcast.14
  420.9 1.0 reduce.2
  421.9 0.1 reshape.29
  422.0 2.1 fusion.6
  424.2 1.2 fusion
  (17 shorter events, 0.2 us)
Async XLA Ops:
  7.2 2.3 copy-start
  7.2 146.4 %copy-start.4 = (bf16[128,1792]{1,0:T(8,128)(2,1)S(1)}, bf16[128,1792]{1,0:T(8,128)(2,1)}, u32[]{:S(2)}) copy-start(bf16[128,1792]{1,0:T(8,128)(2,1)} %param.9) | copy-start | bytes 1376260
  7.2 146.4 %all-gather.3.cloned.1.call-start = ((), (), s32[]{:S(2)}) async-start(), calls=%async_computation.1 | async-start | bytes 14909440 | tf_op jit(solution)/shard_map/all_gather | solution.py:27
  7.9 414.1 %all-gather.5.cloned.1.call-start = ((), (), s32[]{:S(2)}) async-start(), calls=%async_computation.2 | async-start | bytes 1863680 | tf_op jit(solution)/shard_map/all_gather | solution.py:51
  11.0 387.7 %copy-start.2 = (bf16[8,4096]{1,0:T(8,128)(2,1)S(1)}, bf16[8,4096]{1,0:T(8,128)(2,1)}, u32[]{:S(2)}) copy-start(bf16[8,4096]{1,0:T(8,128)(2,1)} %param.7) | copy-start | bytes 196612
  398.7 25.4 %copy-start.3 = (f32[8]{0:T(128)}, f32[8]{0:T(128)S(1)}, u32[]{:S(2)}) copy-start(f32[8]{0:T(128)S(1)} %subtract_divide_fusion) | copy-start | bytes 100
  422.0 2.1 copy-start.1
Sparse Core Ops, SparseCore 0:
  10.2 143.3 all-gather.2
  155.7 118.4 all-gather.4
where the time goes:
time: 433 us; the launch traced here: 432 us
  blocking collectives  255 us (59%)
  waiting for transfers between devices  144 us (33%)
  between operations  15.5 us (4%)
  matrix products  12.9 us (3%)
    all_gather x1, waiting for transfers between devices, local(): lax.all_gather(weight, 'pop', axis=0, tiled=True)  143 us
    psum x1, blocking collectives, local(): mean_reward = lax.psum(jnp.sum(reward), 'pop') / member_count  109 us
    psum x1, blocking collectives, local(): spread = lax.psum(jnp.sum(centered * centered), 'pop') / member_count  105 us
    all_to_all x1, blocking collectives, local(): lax.all_to_all(weighted, 'pop', split_axis=1, concat_axis=0, tiled=True)  21.1 us
    psum x1, blocking collectives, local(): reward = lax.psum(partial_value, 'shard')  20.1 us
  transfers between devices with their start and end apart: 2, of which 1 were waited for; matrix products, arithmetic and copies ran while one was open for 3% of the time, Pallas kernels for 0%

commit v1 on v0

--- a/solution.py
+++ b/solution.py
@@ -24,7 +24,12 @@
     member_count = local_members * lax.axis_size("pop")
     base_out = jnp.dot(
         hidden,
-        lax.all_gather(weight, "pop", axis=0, tiled=True),
+        jnp.concatenate(
+            lax.all_to_all(
+                jnp.stack([weight for _ in range(lax.axis_size("pop"))], 0), "pop", 0, 0
+            ),
+            0,
+        ),
         preferred_element_type=jnp.float32,
     )
     grouped = hidden.reshape(local_members, token_count, feature_count)

time: 433 us -> 959 us (2.21)
  waiting for transfers between devices: 144 us -> 645 us
  starting transfers between devices: 0.08 us -> 18.5 us
    all_to_all x0 -> x1, waiting for transfers between devices: none -> 644 us  [local(): lax.all_to_all(jnp.stack([weight for _ in range(lax.axis_size('pop'))], 0...]
    all_gather x1 -> x0, waiting for transfers between devices: 143 us -> none  [local(): lax.all_gather(weight, 'pop', axis=0, tiled=True)]
    all_to_all x0 -> x1, starting transfers between devices: none -> 18.5 us  [local(): lax.all_to_all(jnp.stack([weight for _ in range(lax.axis_size('pop'))], 0...]
  transfers between devices with their start and end apart: 2 -> 2, of which waited for: 1 -> 1; matrix products, arithmetic and copies ran while one was open for 3% -> 1% of each run, Pallas kernels for 0% -> 0%
where the time goes in v1:
time: 959 us; the launch traced here: 958 us
  waiting for transfers between devices  645 us (67%)
  blocking collectives  256 us (27%)
  starting transfers between devices  18.5 us (2%)
  between operations  15.5 us (2%)
  matrix products  12.1 us (1%)
    all_to_all x1, waiting for transfers between devices, local(): lax.all_to_all(jnp.stack([weight for _ in range(lax.axis_size('pop'))], 0...  644 us
    psum x1, blocking collectives, local(): mean_reward = lax.psum(jnp.sum(reward), 'pop') / member_count  109 us
    psum x1, blocking collectives, local(): spread = lax.psum(jnp.sum(centered * centered), 'pop') / member_count  105 us
    all_to_all x1, blocking collectives, local(): lax.all_to_all(weighted, 'pop', split_axis=1, concat_axis=0, tiled=True)  21.1 us
    psum x1, blocking collectives, local(): reward = lax.psum(partial_value, 'shard')  20.3 us
  transfers between devices with their start and end apart: 2, of which 1 were waited for; matrix products, arithmetic and copies ran while one was open for 1% of the time, Pallas kernels for 0%

profile of v1, /device:TPU:1, one launch (start us, length us, event | category | flops | bytes accessed | tf_op | source)
XLA Modules:
  0.0 958.4 jit_solution(2872921427562330232)
XLA Ops:
  7.2 0.0 copy-start
  7.2 8.0 stack.2
  15.2 18.5 %all-to-all-start = ((bf16[64,64,1792]{2,1,0:T(8,128)(2,1)}), bf16[64,64,1792]{2,1,0:T(8,128)(2,1)}, u32[]{:S(2)}, u32[]{:S(2)}) async-start(bf16[64,64,1792]{2,1,0:T(8,128)(2,1)} %stack.2), calls=%async_computation | async-start | bytes 29360128 | tf_op jit(solution)/shard_map/all_to_all | solution.py:28
  33.7 0.0 all-gather.2.cloned.1.call-start
  33.7 0.7 all-gather.2.cloned.1.call-update
  34.4 0.5 fusion.4
  34.9 644.2 %all-to-all-done = bf16[64,64,1792]{2,1,0:T(8,128)(2,1)} async-done(((bf16[64,64,1792]{2,1,0:T(8,128)(2,1)}), bf16[64,64,1792]{2,1,0:T(8,128)(2,1)}, u32[]{:S(2)}, u32[]{:S(2)}) %all-to-all-start) | async-done | bytes 14680096 | tf_op jit(solution)/shard_map/all_to_all | solution.py:28
  679.1 8.3 fusion.1
  687.4 20.3 %psum.21 = f32[8]{0:T(128)S(1)} all-reduce(f32[8]{0:T(128)S(1)} %get-tuple-element.3), channel_id=1, replica_groups=mesh['pop'=64,'shard'=8] {'shard'}, use_global_device_ids=true, to_apply=%region_1.2 | all-reduce | flops 8 | bytes 64 | tf_op jit(solution)/shard_map/psum | solution.py:47
  707.6 0.6 reduce_sum.28
  708.2 109.4 %psum.22 = f32[]{:T(128)} all-reduce(f32[]{:T(128)} %reduce_sum.28), channel_id=1, replica_groups=mesh['pop'=64,'shard'=8] {'pop'}, use_global_device_ids=true, to_apply=%region_3.4 | all-reduce | flops 1 | bytes 8 | tf_op jit(solution)/shard_map/psum | solution.py:48
  818.3 0.6 multiply_reduce_fusion
  818.9 105.3 %psum.23 = f32[]{:T(128)} all-reduce(f32[]{:T(128)} %multiply_reduce_fusion), channel_id=1, replica_groups=mesh['pop'=64,'shard'=8] {'pop'}, use_global_device_ids=true, to_apply=%region_5.6 | all-reduce | flops 1 | bytes 8 | tf_op jit(solution)/shard_map/psum | solution.py:50
  924.9 0.1 convert_multiply_fusion.1
  925.0 0.1 all_to_all.18
  925.1 0.2 copy.14
  925.3 0.2 reshape.33
  925.5 21.1 %all_to_all.24 = f32[64,1,512]{2,1,0:T(1,128)S(1)} all-to-all(f32[64,1,512]{2,1,0:T(1,128)S(1)} %reshape.33), channel_id=1, replica_groups=mesh['pop'=64,'shard'=8] {'pop'}, dimensions={0} | all-to-all | bytes 262144 | tf_op jit(solution)/shard_map/all_to_all | solution.py:53
  946.6 0.5 broadcast.11
  947.1 0.9 reduce
  948.0 0.1 reshape.34
  948.2 0.0 all-gather.2.cloned.1.call-done
  948.2 2.1 fusion.7
  950.3 1.2 fusion
  (15 shorter events, 0.1 us)
Async XLA Ops:
  7.2 27.2 %copy-start = (bf16[128,4096]{1,0:T(8,128)(2,1)S(1)}, bf16[128,4096]{1,0:T(8,128)(2,1)}, u32[]{:S(2)}) copy-start(bf16[128,4096]{1,0:T(8,128)(2,1)} %param.5) | copy-start | bytes 3145732
  15.2 19.2 %copy-start.3 = (bf16[8,4096]{1,0:T(8,128)(2,1)S(1)}, bf16[8,4096]{1,0:T(8,128)(2,1)}, u32[]{:S(2)}) copy-start(bf16[8,4096]{1,0:T(8,128)(2,1)} %param.7) | copy-start | bytes 196612
  15.2 19.7 %copy-start.2 = (bf16[8,1792]{1,0:T(8,128)(2,1)S(1)}, bf16[8,1792]{1,0:T(8,128)(2,1)}, u32[]{:S(2)}) copy-start(bf16[8,1792]{1,0:T(8,128)(2,1)} %param.8) | copy-start | bytes 86020
  15.2 663.9 %copy-start.5 = (bf16[128,1792]{1,0:T(8,128)(2,1)S(1)}, bf16[128,1792]{1,0:T(8,128)(2,1)}, u32[]{:S(2)}) copy-start(bf16[128,1792]{1,0:T(8,128)(2,1)} %param.9) | copy-start | bytes 1376260
  15.2 663.9 %all-to-all-start = ((bf16[64,64,1792]{2,1,0:T(8,128)(2,1)}), bf16[64,64,1792]{2,1,0:T(8,128)(2,1)}, u32[]{:S(2)}, u32[]{:S(2)}) async-start(bf16[64,64,1792]{2,1,0:T(8,128)(2,1)} %stack.2), calls=%async_computation | async-start | bytes 29360128 | tf_op jit(solution)/shard_map/all_to_all | solution.py:28
  33.7 914.5 %all-gather.2.cloned.1.call-start = ((), (), s32[]{:S(2)}) async-start(), calls=%async_computation.2 | async-start | bytes 1863680 | tf_op jit(solution)/shard_map/all_gather | solution.py:56
  924.9 25.4 %copy-start.4 = (f32[8]{0:T(128)}, f32[8]{0:T(128)S(1)}, u32[]{:S(2)}) copy-start(f32[8]{0:T(128)S(1)} %subtract_divide_fusion) | copy-start | bytes 100
  948.2 2.1 copy-start.1
Sparse Core Ops, SparseCore 0:
  36.6 179.2 all-gather.1
